TPU v7x, 256 devices: a whole 4x4x8 slice. The times are simulated.
256 devices in a mesh: fsdp: 64 (over y, x_hi, z), tensor: 4 (over x_lo, core).
Axes of the slice: x: 4 (x_hi: 2, x_lo: 2; x = x_hi * 2 + x_lo), y: 4, z: 8, core: 2. Of those that a mesh axis runs over, the one named last changes fastest.
Arguments:
- activations: bfloat16 [98304, 5120], P('fsdp', 'tensor'), may hold values from -6 to 6
- key_weight: bfloat16 [5120, 1024], P('tensor'), may hold values from -0.078125 to 0.078125
- key_gain: float32 [128], replicated, may hold values from 0.1 to 1.9
- span_start: int32 [64], P('fsdp'), may hold values from 0 to 4095
- next_weight: bfloat16 [2, 5120, 1024], P(None, ('fsdp', 'tensor')), may hold values from -16 to 16
Outputs:
- new_keys: bfloat16 [98304, 1024], P('fsdp', 'tensor')
- next_scaled: bfloat16 [2, 5120, 1024], P(None, None, 'tensor')
- block_max: float32 [2, 40, 8], P(None, None, 'tensor')
All inputs are finite; a program needn't handle non-finite values. Where the computation divides by a largest or mean magnitude, that divisor is 1e-20 or more.
Results may differ from a plain program's by a relative error of at most 0.015.
Values may be sent and summed in bfloat16 or wider, within the bound.
No kernel may reach another device: no remote copies, remote signals or barrier semaphores. Data moves between devices by JAX's collectives and lax.ppermute only.
A program may use at most 128 MiB of HBM per device.

v0:
```python
import functools
import math

import jax
import jax.numpy as jnp
from jax import lax
from jax.experimental import pallas as pl
from jax.experimental.pallas import tpu as pltpu
from jax.sharding import Mesh
from jax.sharding import PartitionSpec as P

BLOCK = 128
AXES = ("yh", "yl", "xh", "z", "xl", "c")
SIZES = (2, 2, 2, 8, 2, 2)
Y = ("yh", "yl")
F32 = jnp.float32
BF16 = jnp.bfloat16
MIB = 1024 * 1024
NA = 3


after = lax.optimization_barrier


def shift(x, axis, step):
    n = 4 if axis == Y else SIZES[AXES.index(axis)]
    return lax.ppermute(x, axis, [(i, (i + step) % n) for i in range(n)])


def call(kernel, out_shape, flops=0, nbytes=0, vmem=16, **kw):
    return pl.pallas_call(
        kernel,
        out_shape=out_shape,
        compiler_params=pltpu.CompilerParams(vmem_limit_bytes=vmem * MIB),
        cost_estimate=pl.CostEstimate(flops=flops, bytes_accessed=nbytes, transcendentals=0),
        **kw,
    )


VMEM = pl.BlockSpec(memory_space=pltpu.VMEM)


def project_kernel(a, w, pair, mid, own, av, wv, asem, wsem):
    n, rows = av.shape[0], av.shape[1]
    xl, c = lax.axis_index("xl"), lax.axis_index("c")
    tiles = [3 - 2 * xl - c, 2 * xl + 1 - c, 2 - 2 * xl + c, 2 * xl + c]

    def get_w(k):
        at = pl.multiple_of(tiles[k] * 256, 256)
        return pltpu.make_async_copy(w.at[:, pl.ds(at, 256)], wv.at[k], wsem.at[k])

    def get_a(i):
        return pltpu.make_async_copy(a.at[pl.ds(i * rows, rows), :], av.at[i], asem.at[i])

    get_a(0).start()
    for k in range(4):
        get_w(k).start()
    for i in range(1, n):
        get_a(i).start()
    for i in range(n):
        get_a(i).wait()
        at = slice(i * rows, (i + 1) * rows)
        for k, (out, col) in enumerate([(pair, 0), (pair, 256), (mid, 0), (own, 0)]):
            if i == 0:
                get_w(k).wait()
            p = jnp.dot(av[i], wv[k], preferred_element_type=F32)
            out[at, col : col + 256] = p.astype(BF16)


def project(a, w, n=NA):
    t, d = a.shape
    width = w.shape[1] // 4
    hbm = pl.BlockSpec(memory_space=pltpu.HBM)
    return call(
        project_kernel,
        [jax.ShapeDtypeStruct((t, k * width), BF16) for k in (2, 1, 1)],
        flops=8 * t * d * width,
        nbytes=2 * t * d + 8 * d * width + 8 * t * width,
        vmem=58,
        in_specs=[hbm, hbm],
        out_specs=[VMEM] * 3,
        scratch_shapes=[
            pltpu.VMEM((n, t // n, d), BF16),
            pltpu.VMEM((4, d, width), BF16),
            pltpu.SemaphoreType.DMA((n,)),
            pltpu.SemaphoreType.DMA((4,)),
        ],
    )(a, w)


def add_kernel(x, r, out):
    out[...] = (x[...].astype(F32) + r[...].astype(F32)).astype(BF16)


def add(x, r, rows=768):
    t, width = x.shape
    spec = pl.BlockSpec((rows, width), lambda i: (i, 0))
    return call(
        add_kernel,
        jax.ShapeDtypeStruct((t, width), BF16),
        flops=t * width,
        nbytes=6 * t * width,
        grid=(t // rows,),
        in_specs=[spec, pl.BlockSpec((rows, width), lambda i: (i, 0))],
        out_specs=spec,
    )(x, r)


def finish_kernel(own, r1, r2, gain, cosine, sine, out):
    g = gain[...]
    c = cosine[...]
    s = sine[...]
    for h in range(2):
        at = slice(h * 128, (h + 1) * 128)
        x = own[:, at].astype(F32) + r1[:, at].astype(F32) + r2[:, at].astype(F32)
        n = x * lax.rsqrt(jnp.mean(x * x, axis=-1, keepdims=True) + 1e-06) * g
        out[:, at] = (n * c + pltpu.roll(n, 64, 1) * s).astype(BF16)


def finish(own, r1, r2, gain, cosine, sine, rows=768):
    t, width = own.shape
    wide = pl.BlockSpec((rows, width), lambda i: (i, 0))
    narrow = pl.BlockSpec((rows, 128), lambda i: (i, 0))
    return call(
        finish_kernel,
        jax.ShapeDtypeStruct((t, width), BF16),
        flops=20 * t * width,
        nbytes=14 * t * width,
        grid=(t // rows,),
        in_specs=[wide, pl.BlockSpec((rows, width), lambda i: (i, 1)), wide]
        + [pl.BlockSpec((1, 128), lambda i: (0, 0)), narrow, narrow],
        out_specs=wide,
    )(own, r1, r2, gain.reshape(1, 128), cosine, sine)


def tables(span_begin, t):
    lane = jnp.arange(128, dtype=jnp.int32)
    frequency = jnp.exp((lane % 64).astype(F32) * (-2.0 * math.log(1000000.0) / 128))
    k = jnp.arange(t // 32 + 32, dtype=jnp.int32)
    steps = jnp.where(k < t // 32, span_begin + 32 * k, k - t // 32)
    angles = steps.astype(F32)[:, None] * frequency[None, :]
    sign = jnp.where(lane < 64, -1.0, 1.0).astype(F32)
    c, s = lax.optimization_barrier((jnp.cos(angles), jnp.sin(angles)))
    ca, sa = c[: t // 32, None, :], s[: t // 32, None, :]
    cb, sb = c[None, t // 32 :, :], s[None, t // 32 :, :]
    cosine = ca * cb - sa * sb
    sine = (sa * cb + ca * sb) * sign
    return cosine.reshape(t, 128), sine.reshape(t, 128)


def spread_kernel(w, out):
    x = w[...].astype(F32)
    rows = jnp.concatenate([x[:, 0, :], x[:, 1, :]], axis=0).astype(BF16)
    for k in range(4):
        for t in range(4):
            out[k * 4 + t] = rows[:, t * 256 : (t + 1) * 256]


def fold(x):
    wide = jnp.concatenate([x[:40], x[40:]], axis=1)
    return jnp.concatenate([wide, jnp.zeros((8, 256), F32)], axis=0)


def unfold(x):
    return jnp.concatenate([x[:40, :128], x[:40, 128:]], axis=0)


def merge_kernel(x, outa, outb):
    mine = lax.axis_index("yl") * 8
    for xh in range(2):
        lines = [x[mine + xh * 4 + t].astype(F32) for t in range(4)]
        one, two = (
            jnp.concatenate([line[k * 20 : k * 20 + 20] for line in lines], axis=0)
            for k in range(2)
        )
        outa[xh * 80 : xh * 80 + 80, :] = one.astype(BF16)
        if xh == 1:
            outa[160:208, :] = fold(two[:, 128:]).astype(BF16)
    for yl in range(2):
        for xh in range(2):
            lines = [x[yl * 8 + xh * 4 + t].astype(F32) for t in range(4)]
            two = jnp.concatenate([line[20:40] for line in lines], axis=0)
            if xh == 0:
                outb[yl * 128 : yl * 128 + 80, :] = two.astype(BF16)
            else:
                outb[yl * 128 + 80 : yl * 128 + 128, :] = fold(two[:, :128]).astype(BF16)


def stack_kernel(own, other, out):
    yh = lax.axis_index("yh")
    for d, ref in enumerate((own, other)):
        for yl in range(2):
            at = lax.rem(yh + d, 2) * 2 + yl
            out[pl.ds(pl.multiple_of(at * 80, 16), 80), :] = ref[yl * 128 : yl * 128 + 80, :]
            col = pl.multiple_of(at // 2 * 128, 128)
            side = unfold(ref[yl * 128 + 80 : yl * 128 + 128, :].astype(F32))
            out[320 + yl * 80 : 400 + yl * 80, pl.ds(col, 128)] = side.astype(BF16)


def rows_kernel(*refs):
    z = lax.axis_index("z")
    out = refs[-1]
    for d in range(8):
        at = lax.rem(z + d, 8)
        for h in range(2):
            row = pl.multiple_of(320 + at * 80 + h * 640, 16)
            out[pl.ds(row, 80), :] = refs[d][h * 80 : h * 80 + 80, :]
        row = pl.multiple_of(lax.rem(at, 4) * 80, 16)
        col = pl.multiple_of(at // 4 * 128, 128)
        out[pl.ds(row, 80), pl.ds(col, 128)] = unfold(refs[d][160:208, :].astype(F32)).astype(BF16)


def small(kernel, shapes, *arrays):
    single = len(shapes) == 1
    out = [jax.ShapeDtypeStruct(s, BF16) for s in shapes]
    return call(
        kernel,
        out[0] if single else out,
        nbytes=4 * sum(math.prod(s) for s in shapes),
        in_specs=[VMEM] * len(arrays),
        out_specs=VMEM if single else [VMEM] * len(out),
    )(*arrays)


def scale_blocks(x, start, count, first, put, bm):
    lane = lax.broadcasted_iota(jnp.int32, (1, 128), 1)
    for j in range(2):
        row = bm[j : j + 1, :]
        for k in range(count // 128):
            blk = x[start + k * 128 : start + (k + 1) * 128, j * 128 : (j + 1) * 128]
            top = jnp.max(jnp.abs(blk), axis=0, keepdims=True).astype(F32)
            m = jnp.max(top, axis=1, keepdims=True) + 1e-06
            put(k, j, (blk.astype(F32) * (1.0 / m)).astype(BF16))
            row = jnp.where(lane == first + k, m, row)
        bm[j : j + 1, :] = row


def y_at(offsets, i):
    d = offsets[0]
    for u, other in enumerate(offsets[1:], 1):
        d = jnp.where(i == u, other, d)
    return lax.rem(lax.axis_index(Y) + d, 4)


def scale_groups_kernel(groups, offsets, n, *refs):
    ins, out, bm = refs[:n], refs[-2], refs[-1]
    i = pl.program_id(0)
    y = lax.axis_index(Y)

    @pl.when(i == 0)
    def _():
        bm[...] = refs[n][...] if len(refs) > n + 2 else jnp.zeros_like(bm)

    for u, group in enumerate(groups):

        @pl.when(i == u)
        def _(u=u, group=group):
            row = 0
            for k, start, count in group:
                base = row

                def put(r, j, v):
                    out[0, base + r * 128 : base + (r + 1) * 128, j * 128 : (j + 1) * 128] = v

                first = lax.rem(y + offsets[u], 4) * 10 + row // 128
                scale_blocks(ins[k], start, count, first, put, bm)
                row += count


def scale_groups(pieces, groups, offsets, done=None):
    n = len(pieces)
    ins = list(pieces)
    alias = {}
    if done is not None:
        ins += [done[1], done[0]]
        alias = {n + 1: 0, n: 1}
    in_specs = [pl.BlockSpec(p.shape, lambda i: (0, 0)) for p in ins[: n + 1]]
    if done is not None:
        in_specs.append(pl.BlockSpec(memory_space=pl.ANY))
    return call(
        functools.partial(scale_groups_kernel, groups, offsets, n),
        [jax.ShapeDtypeStruct((2, 5120, 256), BF16), jax.ShapeDtypeStruct((2, 128), F32)],
        flops=len(groups) * 1280 * 256 * 8,
        nbytes=len(groups) * 1280 * 256 * 4,
        grid=(len(groups),),
        in_specs=in_specs,
        out_specs=[
            pl.BlockSpec((1, 1280, 256), lambda i: (0, y_at(offsets, i), 0)),
            pl.BlockSpec((2, 128), lambda i: (0, 0)),
        ],
        input_output_aliases=alias,
    )(*ins)


def scale_last_kernel(*refs):
    z, y = lax.axis_index("z"), lax.axis_index(Y)
    whole, half, low, high, part, extra = refs[:7], refs[7:14], *refs[14:17], refs[17:20]
    far0, far1, bma, _, out, bm, held, acc, acc0 = refs[20:]
    i = pl.program_id(0)

    def put(r, j, v):
        out[0, r * 128 : (r + 1) * 128, j * 128 : (j + 1) * 128] = v

    def row(d):
        return pl.multiple_of(lax.rem(z + d, 8) * 80, 16)

    def place(d, ref):
        held[pl.ds(row(d), 80), :] = ref[...]

    @pl.when(i == 0)
    def _():
        acc[...] = jnp.zeros_like(acc)
        acc0[...] = bma[...]

    @pl.when(i < 4)
    def _():
        col = pl.multiple_of(i // 2 * 128, 128)
        for d, ref, side in zip((0, 1, 2, 3, 5, 6, 7), whole, half):
            place(d, ref)
            held[pl.ds(row(d) + 640, 80), 0:128] = side[:, pl.ds(col, 128)]
        held[pl.ds(row(4) + 640, 80), 0:128] = part[:, pl.ds(col, 128)]

    @pl.when(i < 3)
    def _():
        place(4, low)

    @pl.when(i == 3)
    def _():
        place(4, high)

    for d, ref in zip((0, 1, 2, 3), (extra[0], extra[1], far0, extra[2])):

        @pl.when((lax.rem(y + d, 4) == i) & (i < 4))
        def _(ref=ref):
            held[640:960, 128:256] = ref[0:320, 0:128]
            held[960:1280, 128:256] = ref[0:320, 128:256]

    @pl.when(i < 4)
    def _():
        scale_blocks(held, 0, 1280, i * 10, put, acc)

    @pl.when(i == 4)
    def _():
        held[0:480, :] = far0[320:800, :]
        held[480:1280, :] = far1[...]
        scale_blocks(held, 0, 1280, lax.rem(y + 2, 4) * 10, put, acc0)
        bm[0] = acc0[:, :40]
        bm[1] = acc[:, :40]


def scale_last(pieces, low, high, extra, far0, far1, done):
    part = (80, 256)
    at = lambda i: jnp.minimum(i, 3)
    return call(
        scale_last_kernel,
        [jax.ShapeDtypeStruct((2, 5120, 256), BF16), jax.ShapeDtypeStruct((2, 2, 40), F32)],
        flops=6400 * 256 * 8,
        nbytes=6400 * 256 * 4,
        grid=(5,),
        in_specs=[pl.BlockSpec(part, lambda i: (at(i), 0))] * 7
        + [pl.BlockSpec(part, lambda i: (4 + lax.rem(at(i), 2), 0))] * 7
        + [
            pl.BlockSpec(part, lambda i: (jnp.minimum(i, 2), 0)),
            pl.BlockSpec(part, lambda i: (0, 0)),
            pl.BlockSpec(part, lambda i: (1 + lax.rem(at(i), 2), 0)),
        ]
        + [pl.BlockSpec((320, 256), lambda i: (0, 0))] * 3
        + [pl.BlockSpec((800, 256), lambda i: (0, 0))] * 2
        + [
            pl.BlockSpec((2, 128), lambda i: (0, 0)),
            pl.BlockSpec(memory_space=pl.ANY),
        ],
        out_specs=[
            pl.BlockSpec(
                (1, 1280, 256),
                lambda i: (
                    jnp.where(i < 4, 1, 0),
                    jnp.where(i < 4, i, lax.rem(lax.axis_index(Y) + 2, 4)),
                    0,
                ),
            ),
            pl.BlockSpec((2, 2, 40), lambda i: (0, 0, 0)),
        ],
        scratch_shapes=[
            pltpu.VMEM((1280, 256), BF16),
            pltpu.VMEM((2, 128), F32),
            pltpu.VMEM((2, 128), F32),
        ],
        input_output_aliases={23: 0},
    )(*pieces, *pieces, low, high, high, *extra, far0, far1, done[1], done[0])


def body(activations, key_weight, key_gain, span_start, next_weight):
    line = small(spread_kernel, [(16, 40, 256)], next_weight.transpose(1, 0, 2))
    line = lax.all_to_all(line, ("yl", "xh", "xl", "c"), split_axis=0, concat_axis=0, tiled=True)
    pair, mid, own = project(activations, key_weight)
    line, pair = after((line, pair))
    a0, b0 = small(merge_kernel, [(208, 256), (256, 256)], line)

    az = {0: a0}
    az[1], az[7] = shift(a0, "z", -1), shift(a0, "z", 1)
    other = shift(b0, "yh", 1)
    az[2], az[6] = shift(az[1], "z", -1), shift(az[7], "z", 1)
    az[3], az[5] = shift(az[2], "z", -1), shift(az[6], "z", 1)
    az[4] = shift(az[3], "z", -1)
    mb = small(stack_kernel, [(480, 256)], b0, other)
    ma = small(rows_kernel, [(1600, 256)], *[az[d] for d in range(8)])
    mb, ma, pair = after((mb, ma, pair))

    bz = {0: mb}
    bz[1], bz[7] = shift(mb, "z", -1), shift(mb, "z", 1)
    up, down = shift(ma, Y, -1), shift(ma, Y, 1)
    r1 = shift(pair, "c", 1)
    half = add(mid, r1)
    bz[1], bz[7], half = after((bz[1], bz[7], half))
    r2 = shift(half, "xl", 1)
    bz[2], bz[6] = shift(bz[1], "z", -1), shift(bz[7], "z", 1)
    done = scale_groups([ma], [[(0, 320, 1280)]], [0])
    bz[2], bz[6], *done = after((bz[2], bz[6], *done))
    bz[3], bz[5] = shift(bz[2], "z", -1), shift(bz[6], "z", 1)
    far0 = shift(up[:800], Y, -1)
    far1 = shift(down[800:], Y, 1)
    done = scale_groups([up, down], [[(0, 320, 1280)], [(1, 320, 1280)]], [1, 3], done)
    bz[3], bz[5], *done = after((bz[3], bz[5], *done))
    low = shift(bz[3][:240], "z", -1)
    high = shift(bz[5][240:], "z", 1)
    cosine, sine = tables(span_start[0], activations.shape[0])
    new_keys = finish(own, r1, r2, key_gain, cosine, sine)
    low, high, far0, far1, new_keys, *done = after((low, high, far0, far1, new_keys, *done))
    pieces = [bz[d] for d in (0, 1, 2, 3, 5, 6, 7)]
    next_scaled, block_max = scale_last(pieces, low, high, [ma, up, down], far0, far1, done)
    return new_keys, next_scaled, block_max.transpose(0, 2, 1)


def solution(mesh):
    line = Mesh(mesh.devices.reshape(SIZES), AXES)
    fsdp, tensor = (*Y, "xh", "z"), ("xl", "c")
    placed = (
        P(fsdp, tensor),
        P(tensor, None),
        P(),
        P(fsdp),
        P(None, fsdp + tensor, None),
    )
    return jax.shard_map(
        body,
        mesh=line,
        in_specs=placed,
        out_specs=(P(fsdp, tensor), P(None, None, tensor), P(None, None, tensor)),
        check_vma=False,
    )
```

profile of v0, /device:TPU:26, one launch (start us, length us, event | category | flops | bytes accessed | tf_op | source)
XLA Modules:
  0.0 86.0 jit_solution(3529454168074809990)
XLA Ops:
  0.6 0.9 %copy-done.2 = bf16[2,20,1024]{2,0,1:T(2,128)(2,1)S(1)} copy-done((bf16[2,20,1024]{2,0,1:T(2,128)(2,1)S(1)}, bf16[2,20,1024]{2,0,1:T(2,128)(2,1)}, u32[]{:S(2)}) %copy-start.2) | copy-done | bytes 81944
  1.5 0.8 shard_map.76
  2.3 5.8 %all-to-all-start = ((bf16[16,40,256]{2,1,0:T(8,128)(2,1)}), bf16[16,40,256]{2,1,0:T(8,128)(2,1)S(1)}, u32[]{:S(2)}, u32[]{:S(2)}) async-start(bf16[16,40,256]{2,1,0:T(8,128)(2,1)} %shard_map.76), calls=%async_computation | async-start | bytes 655360 | tf_op jit(solution)/shard_map/all_to_all | solution.py:395
  8.1 9.1 %shard_map.77 = (bf16[1536,512]{1,0:T(8,128)(2,1)}, bf16[1536,256]{1,0:T(8,128)(2,1)}, bf16[1536,256]{1,0:T(8,128)(2,1)}) custom-call(bf16[1536,1280]{1,0:T(8,128)(2,1)} %a.1, bf16[1280,1024]{1,0:T(8,128)(2,1)} %w.1), custom_call_target="tpu_custom_call" | custom-call | flops 4026531840 | bytes 9699328 | tf_op jit(solution)/shard_map/pallas_call | solution.py:74
  17.2 5.9 %collective-permute-start.1 = (bf16[208,256]{1,0:T(8,128)(2,1)S(1)}, bf16[208,256]{1,0:T(8,128)(2,1)S(1)}, u32[]{:S(2)}, u32[]{:S(2)}) collective-permute-start(bf16[208,256]{1,0:T(8,128)(2,1)S(1)} %get-tuple-element.42.refs_0_), channel_id=1, source_target_pairs={{0,28},{4,0},{8,4},{12,8},{16,12},{20,16},{24,20},{28,24},{1,29},{... | collective-permute-start | bytes 319496 | tf_op jit(solution)/shard_map/ppermute | solution.py:27
  23.1 2.5 %collective-permute-done.1.refs_1_ = bf16[208,256]{1,0:T(8,128)(2,1)S(1)} collective-permute-done((bf16[208,256]{1,0:T(8,128)(2,1)S(1)}, bf16[208,256]{1,0:T(8,128)(2,1)S(1)}, u32[]{:S(2)}, u32[]{:S(2)}) %collective-permute-start.1) | collective-permute-done | bytes 106528 | tf_op jit(solution)/shard_map/ppermute | solution.py:27
  25.6 3.7 %collective-permute-start.2 = (bf16[208,256]{1,0:T(8,128)(2,1)S(1)}, bf16[208,256]{1,0:T(8,128)(2,1)S(1)}, u32[]{:S(2)}, u32[]{:S(2)}) collective-permute-start(bf16[208,256]{1,0:T(8,128)(2,1)S(1)} %collective-permute-done.1.refs_1_), channel_id=1, source_target_pairs={{0,28},{4,0},{8,4},{12,8},{16,12},{20,16},{24,20},{28,24},{1,29},{... | collective-permute-start | bytes 319496 | tf_op jit(solution)/shard_map/ppermute | solution.py:27
  29.3 2.3 %collective-permute-done.2.refs_2_ = bf16[208,256]{1,0:T(8,128)(2,1)S(1)} collective-permute-done((bf16[208,256]{1,0:T(8,128)(2,1)S(1)}, bf16[208,256]{1,0:T(8,128)(2,1)S(1)}, u32[]{:S(2)}, u32[]{:S(2)}) %collective-permute-start.2) | collective-permute-done | bytes 106528 | tf_op jit(solution)/shard_map/ppermute | solution.py:27
  31.6 3.6 %collective-permute-start.3 = (bf16[208,256]{1,0:T(8,128)(2,1)S(1)}, bf16[208,256]{1,0:T(8,128)(2,1)S(1)}, u32[]{:S(2)}, u32[]{:S(2)}) collective-permute-start(bf16[208,256]{1,0:T(8,128)(2,1)S(1)} %collective-permute-done.2.refs_2_), channel_id=1, source_target_pairs={{0,28},{4,0},{8,4},{12,8},{16,12},{20,16},{24,20},{28,24},{1,29},{... | collective-permute-start | bytes 319496 | tf_op jit(solution)/shard_map/ppermute | solution.py:27
  35.3 1.2 %collective-permute-start = (bf16[256,256]{1,0:T(8,128)(2,1)S(1)}, bf16[256,256]{1,0:T(8,128)(2,1)S(1)}, u32[]{:S(2)}, u32[]{:S(2)}) collective-permute-start(bf16[256,256]{1,0:T(8,128)(2,1)S(1)} %get-tuple-element.41.own), channel_id=1, source_target_pairs={{0,128},{128,0},{1,129},{129,1},{2,130},{130,2},{3,131},{131,3},{4... | collective-permute-start | bytes 393224 | tf_op jit(solution)/shard_map/ppermute | solution.py:27
  36.5 1.0 %collective-permute-done.3.refs_3_ = bf16[208,256]{1,0:T(8,128)(2,1)S(1)} collective-permute-done((bf16[208,256]{1,0:T(8,128)(2,1)S(1)}, bf16[208,256]{1,0:T(8,128)(2,1)S(1)}, u32[]{:S(2)}, u32[]{:S(2)}) %collective-permute-start.3) | collective-permute-done | bytes 106528 | tf_op jit(solution)/shard_map/ppermute | solution.py:27
  37.5 3.6 %collective-permute-start.4 = (bf16[208,256]{1,0:T(8,128)(2,1)S(1)}, bf16[208,256]{1,0:T(8,128)(2,1)S(1)}, u32[]{:S(2)}, u32[]{:S(2)}) collective-permute-start(bf16[208,256]{1,0:T(8,128)(2,1)S(1)} %collective-permute-done.3.refs_3_), channel_id=1, source_target_pairs={{0,28},{4,0},{8,4},{12,8},{16,12},{20,16},{24,20},{28,24},{1,29},{... | collective-permute-start | bytes 319496 | tf_op jit(solution)/shard_map/ppermute | solution.py:27
  42.4 1.1 %collective-permute-done.4.refs_4_ = bf16[208,256]{1,0:T(8,128)(2,1)S(1)} collective-permute-done((bf16[208,256]{1,0:T(8,128)(2,1)S(1)}, bf16[208,256]{1,0:T(8,128)(2,1)S(1)}, u32[]{:S(2)}, u32[]{:S(2)}) %collective-permute-start.4) | collective-permute-done | bytes 106528 | tf_op jit(solution)/shard_map/ppermute | solution.py:27
  43.8 3.7 %collective-permute-start.8 = (bf16[480,256]{1,0:T(8,128)(2,1)S(1)}, bf16[480,256]{1,0:T(8,128)(2,1)S(1)}, u32[]{:S(2)}, u32[]{:S(2)}) collective-permute-start(bf16[480,256]{1,0:T(8,128)(2,1)S(1)} %shard_map.79.refs_0_.refs_7_), channel_id=1, source_target_pairs={{0,28},{4,0},{8,4},{12,8},{16,12},{20,16},{24,20},{28,24},{1,29},{... | collective-permute-start | bytes 737288 | tf_op jit(solution)/shard_map/ppermute | solution.py:27
  48.1 0.8 collective-permute-start.16
  48.9 1.5 %collective-permute-start.15 = (bf16[1600,256]{1,0:T(8,128)(2,1)S(1)}, bf16[1600,256]{1,0:T(8,128)(2,1)S(1)}, u32[]{:S(2)}, u32[]{:S(2)}) collective-permute-start(bf16[1600,256]{1,0:T(8,128)(2,1)S(1)} %shard_map.80.refs_0_.refs_17_), channel_id=1, source_target_pairs={{0,192},{64,0},{128,64},{192,128},{1,193},{65,1},{129,65},{193,129... | collective-permute-start | bytes 2457608 | tf_op jit(solution)/shard_map/ppermute | solution.py:27
  50.4 1.1 %copy-done = bf16[1536,256]{1,0:T(8,128)(2,1)S(1)} copy-done((bf16[1536,256]{1,0:T(8,128)(2,1)S(1)}, bf16[1536,256]{1,0:T(8,128)(2,1)}, u32[]{:S(2)}) %copy-start) | copy-done | bytes 786456
  51.8 2.1 %collective-permute-done.9.refs_6_.refs_13_ = bf16[480,256]{1,0:T(8,128)(2,1)S(1)} collective-permute-done((bf16[480,256]{1,0:T(8,128)(2,1)S(1)}, bf16[480,256]{1,0:T(8,128)(2,1)S(1)}, u32[]{:S(2)}, u32[]{:S(2)}) %collective-permute-start.9) | collective-permute-done | bytes 245792 | tf_op jit(solution)/shard_map/ppermute | solution.py:27
  53.9 3.0 %collective-permute-start.11 = (bf16[480,256]{1,0:T(8,128)(2,1)S(1)}, bf16[480,256]{1,0:T(8,128)(2,1)S(1)}, u32[]{:S(2)}, u32[]{:S(2)}) collective-permute-start(bf16[480,256]{1,0:T(8,128)(2,1)S(1)} %collective-permute-done.8.refs_1_.refs_8_), channel_id=1, source_target_pairs={{0,28},{4,0},{8,4},{12,8},{16,12},{20,16},{24,20},{28,24},{1,29},{... | collective-permute-start | bytes 737288 | tf_op jit(solution)/shard_map/ppermute | solution.py:27
  57.1 0.6 collective-permute-start.21
  57.8 1.1 %shard_map.82 = (bf16[2,5120,256]{2,1,0:T(8,128)(2,1)}, f32[2,128]{1,0:T(2,128)S(1)}) custom-call(bf16[1600,256]{1,0:T(8,128)(2,1)S(1)} %shard_map.80.refs_0_.refs_17_), custom_call_target="tpu_custom_call" | custom-call | flops 2621440 | bytes 1310720 | tf_op jit(solution)/shard_map/pallas_call | solution.py:280
  58.9 2.9 %collective-permute-done.11.refs_2_.refs_9_ = bf16[480,256]{1,0:T(8,128)(2,1)S(1)} collective-permute-done((bf16[480,256]{1,0:T(8,128)(2,1)S(1)}, bf16[480,256]{1,0:T(8,128)(2,1)S(1)}, u32[]{:S(2)}, u32[]{:S(2)}) %collective-permute-start.11) | collective-permute-done | bytes 245792 | tf_op jit(solution)/shard_map/ppermute | solution.py:27
  61.8 3.4 %collective-permute-done.12.refs_5_.refs_12_ = bf16[480,256]{1,0:T(8,128)(2,1)S(1)} collective-permute-done((bf16[480,256]{1,0:T(8,128)(2,1)S(1)}, bf16[480,256]{1,0:T(8,128)(2,1)S(1)}, u32[]{:S(2)}, u32[]{:S(2)}) %collective-permute-start.12) | collective-permute-done | bytes 245792 | tf_op jit(solution)/shard_map/ppermute | solution.py:27
  65.5 1.7 %collective-permute-start.14 = (bf16[480,256]{1,0:T(8,128)(2,1)S(1)}, bf16[480,256]{1,0:T(8,128)(2,1)S(1)}, u32[]{:S(2)}, u32[]{:S(2)}) collective-permute-start(bf16[480,256]{1,0:T(8,128)(2,1)S(1)} %collective-permute-done.12.refs_5_.refs_12_), channel_id=1, source_target_pairs={{0,4},{4,8},{8,12},{12,16},{16,20},{20,24},{24,28},{28,0},{1,5},{5... | collective-permute-start | bytes 737288 | tf_op jit(solution)/shard_map/ppermute | solution.py:27
  67.5 1.1 %collective-permute-done.16.refs_1_.refs_19_ = bf16[1600,256]{1,0:T(8,128)(2,1)S(1)} collective-permute-done((bf16[1600,256]{1,0:T(8,128)(2,1)S(1)}, bf16[1600,256]{1,0:T(8,128)(2,1)S(1)}, u32[]{:S(2)}, u32[]{:S(2)}) %collective-permute-start.16) | collective-permute-done | bytes 819232 | tf_op jit(solution)/shard_map/ppermute | solution.py:27
  68.6 1.8 %collective-permute-start.20 = (bf16[800,256]{1,0:T(8,128)(2,1)S(1)}, bf16[800,256]{1,0:T(8,128)(2,1)S(1)}, u32[]{:S(2)}, u32[]{:S(2)}) collective-permute-start(bf16[800,256]{1,0:T(8,128)(2,1)S(1)} %slice.33), channel_id=1, source_target_pairs={{0,64},{64,128},{128,192},{192,0},{1,65},{65,129},{129,193},{193,1... | collective-permute-start | bytes 1228808 | tf_op jit(solution)/shard_map/ppermute | solution.py:27
  70.8 1.5 %shard_map.83 = (bf16[2,5120,256]{2,1,0:T(8,128)(2,1)}, f32[2,128]{1,0:T(2,128)S(1)}) custom-call(bf16[1600,256]{1,0:T(8,128)(2,1)S(1)} %collective-permute-done.15.refs_0_.refs_18_, bf16[1600,256]{1,0:T(8,128)(2,1)S(1)} %collective-permute-done.16.refs_1_.refs_19_, ...), custom_call_target="tpu_custom_call", output_to_operand_aliasing={{0}: (3, {}), {1}: (2, {})} | custom-call | flops 5242880 | bytes 2621440 | tf_op jit(solution)/shard_map/pallas_call | solution.py:280
  73.5 2.7 %collective-permute-start.17 = (bf16[240,256]{1,0:T(8,128)(2,1)S(1)}, bf16[240,256]{1,0:T(8,128)(2,1)S(1)}, u32[]{:S(2)}, u32[]{:S(2)}) collective-permute-start(bf16[240,256]{1,0:T(8,128)(2,1)S(1)} %slice.24), channel_id=1, source_target_pairs={{0,28},{4,0},{8,4},{12,8},{16,12},{20,16},{24,20},{28,24},{1,29},{... | collective-permute-start | bytes 368648 | tf_op jit(solution)/shard_map/ppermute | solution.py:27
  76.3 2.0 %shard_map.84 = bf16[1536,256]{1,0:T(8,128)(2,1)} custom-call(bf16[1536,256]{1,0:T(8,128)(2,1)S(1)} %copy-done.1, bf16[1536,512]{1,0:T(8,128)(2,1)S(1)} %collective-permute-done.10.r.r1, bf16[1536,256]{1,0:T(8,128)(2,1)S(1)} %collective-permute-done.21.r2, f32[1,128]{1,0:T(1,128)S(1)} %bitcast.10, f32[1536,128]{1,0:T(8,128)S(1)} %bitcast.8, ...), custom_call_target="tpu_custom_call" | custom-call | flops 7864320 | bytes 5505024 | tf_op jit(solution)/shard_map/pallas_call | solution.py:124
  78.3 1.0 %collective-permute-done.20.refs_21_ = bf16[800,256]{1,0:T(8,128)(2,1)S(1)} collective-permute-done((bf16[800,256]{1,0:T(8,128)(2,1)S(1)}, bf16[800,256]{1,0:T(8,128)(2,1)S(1)}, u32[]{:S(2)}, u32[]{:S(2)}) %collective-permute-start.20) | collective-permute-done | bytes 409632 | tf_op jit(solution)/shard_map/ppermute | solution.py:27
  79.3 2.8 %collective-permute-done.19.refs_20_ = bf16[800,256]{1,0:T(8,128)(2,1)S(1)} collective-permute-done((bf16[800,256]{1,0:T(8,128)(2,1)S(1)}, bf16[800,256]{1,0:T(8,128)(2,1)S(1)}, u32[]{:S(2)}, u32[]{:S(2)}) %collective-permute-start.19) | collective-permute-done | bytes 409632 | tf_op jit(solution)/shard_map/ppermute | solution.py:27
  82.1 3.8 %shard_map.85 = (bf16[2,5120,256]{2,1,0:T(8,128)(2,1)}, f32[2,2,40]{2,1,0:T(2,128)}) custom-call(bf16[480,256]{1,0:T(8,128)(2,1)S(1)} %shard_map.79.refs_0_.refs_7_, bf16[480,256]{1,0:T(8,128)(2,1)S(1)} %collective-permute-done.8.refs_1_.refs_8_, bf16[480,256]{1,0:T(8,128)(2,1)S(1)} %collective-permute-done.11.refs_2_.refs_9_, ...), custom_call_target="tpu_custom_call", output_to_operand_aliasing={{0}: (23, {})} | custom-call | flops 13107200 | bytes 6553600 | tf_op jit(solution)/shard_map/pallas_call | solution.py:354
  (46 shorter events, 4.3 us)
Async XLA Ops:
  0.6 0.9 %copy-start.2 = (bf16[2,20,1024]{2,0,1:T(2,128)(2,1)S(1)}, bf16[2,20,1024]{2,0,1:T(2,128)(2,1)}, u32[]{:S(2)}) copy-start(bf16[2,20,1024]{2,0,1:T(2,128)(2,1)} %param.9) | copy-start | bytes 245764
  2.3 14.8 %all-to-all-start = ((bf16[16,40,256]{2,1,0:T(8,128)(2,1)}), bf16[16,40,256]{2,1,0:T(8,128)(2,1)S(1)}, u32[]{:S(2)}, u32[]{:S(2)}) async-start(bf16[16,40,256]{2,1,0:T(8,128)(2,1)} %shard_map.76), calls=%async_computation | async-start | bytes 655360 | tf_op jit(solution)/shard_map/all_to_all | solution.py:395
  17.2 8.5 %collective-permute-start.1 = (bf16[208,256]{1,0:T(8,128)(2,1)S(1)}, bf16[208,256]{1,0:T(8,128)(2,1)S(1)}, u32[]{:S(2)}, u32[]{:S(2)}) collective-permute-start(bf16[208,256]{1,0:T(8,128)(2,1)S(1)} %get-tuple-element.42.refs_0_), channel_id=1, source_target_pairs={{0,28},{4,0},{8,4},{12,8},{16,12},{20,16},{24,20},{28,24},{1,29},{... | collective-permute-start | bytes 319496 | tf_op jit(solution)/shard_map/ppermute | solution.py:27
  23.1 6.2 %collective-permute-start.5 = (bf16[208,256]{1,0:T(8,128)(2,1)S(1)}, bf16[208,256]{1,0:T(8,128)(2,1)S(1)}, u32[]{:S(2)}, u32[]{:S(2)}) collective-permute-start(bf16[208,256]{1,0:T(8,128)(2,1)S(1)} %get-tuple-element.42.refs_0_), channel_id=1, source_target_pairs={{0,4},{4,8},{8,12},{12,16},{16,20},{20,24},{24,28},{28,0},{1,5},{5... | collective-permute-start | bytes 319496 | tf_op jit(solution)/shard_map/ppermute | solution.py:27
  25.6 6.0 %collective-permute-start.2 = (bf16[208,256]{1,0:T(8,128)(2,1)S(1)}, bf16[208,256]{1,0:T(8,128)(2,1)S(1)}, u32[]{:S(2)}, u32[]{:S(2)}) collective-permute-start(bf16[208,256]{1,0:T(8,128)(2,1)S(1)} %collective-permute-done.1.refs_1_), channel_id=1, source_target_pairs={{0,28},{4,0},{8,4},{12,8},{16,12},{20,16},{24,20},{28,24},{1,29},{... | collective-permute-start | bytes 319496 | tf_op jit(solution)/shard_map/ppermute | solution.py:27
  29.3 7.2 %collective-permute-start.6 = (bf16[208,256]{1,0:T(8,128)(2,1)S(1)}, bf16[208,256]{1,0:T(8,128)(2,1)S(1)}, u32[]{:S(2)}, u32[]{:S(2)}) collective-permute-start(bf16[208,256]{1,0:T(8,128)(2,1)S(1)} %collective-permute-done.5.refs_7_), channel_id=1, source_target_pairs={{0,4},{4,8},{8,12},{12,16},{16,20},{20,24},{24,28},{28,0},{1,5},{5... | collective-permute-start | bytes 319496 | tf_op jit(solution)/shard_map/ppermute | solution.py:27
  31.6 5.9 %collective-permute-start.3 = (bf16[208,256]{1,0:T(8,128)(2,1)S(1)}, bf16[208,256]{1,0:T(8,128)(2,1)S(1)}, u32[]{:S(2)}, u32[]{:S(2)}) collective-permute-start(bf16[208,256]{1,0:T(8,128)(2,1)S(1)} %collective-permute-done.2.refs_2_), channel_id=1, source_target_pairs={{0,28},{4,0},{8,4},{12,8},{16,12},{20,16},{24,20},{28,24},{1,29},{... | collective-permute-start | bytes 319496 | tf_op jit(solution)/shard_map/ppermute | solution.py:27
  35.3 6.5 %collective-permute-start = (bf16[256,256]{1,0:T(8,128)(2,1)S(1)}, bf16[256,256]{1,0:T(8,128)(2,1)S(1)}, u32[]{:S(2)}, u32[]{:S(2)}) collective-permute-start(bf16[256,256]{1,0:T(8,128)(2,1)S(1)} %get-tuple-element.41.own), channel_id=1, source_target_pairs={{0,128},{128,0},{1,129},{129,1},{2,130},{130,2},{3,131},{131,3},{4... | collective-permute-start | bytes 393224 | tf_op jit(solution)/shard_map/ppermute | solution.py:27
  36.5 5.9 %collective-permute-start.7 = (bf16[208,256]{1,0:T(8,128)(2,1)S(1)}, bf16[208,256]{1,0:T(8,128)(2,1)S(1)}, u32[]{:S(2)}, u32[]{:S(2)}) collective-permute-start(bf16[208,256]{1,0:T(8,128)(2,1)S(1)} %collective-permute-done.6.refs_6_), channel_id=1, source_target_pairs={{0,4},{4,8},{8,12},{12,16},{16,20},{20,24},{24,28},{28,0},{1,5},{5... | collective-permute-start | bytes 319496 | tf_op jit(solution)/shard_map/ppermute | solution.py:27
  37.5 5.9 %collective-permute-start.4 = (bf16[208,256]{1,0:T(8,128)(2,1)S(1)}, bf16[208,256]{1,0:T(8,128)(2,1)S(1)}, u32[]{:S(2)}, u32[]{:S(2)}) collective-permute-start(bf16[208,256]{1,0:T(8,128)(2,1)S(1)} %collective-permute-done.3.refs_3_), channel_id=1, source_target_pairs={{0,28},{4,0},{8,4},{12,8},{16,12},{20,16},{24,20},{28,24},{1,29},{... | collective-permute-start | bytes 319496 | tf_op jit(solution)/shard_map/ppermute | solution.py:27
  43.6 6.8 %collective-permute-start.10 = (bf16[1536,512]{1,0:T(8,128)(2,1)}, bf16[1536,512]{1,0:T(8,128)(2,1)S(1)}, u32[]{:S(2)}, u32[]{:S(2)}) collective-permute-start(bf16[1536,512]{1,0:T(8,128)(2,1)} %get-tuple-element.46), channel_id=1, source_target_pairs={{0,1},{1,0},{2,3},{3,2},{4,5},{5,4},{6,7},{7,6},{8,9},{9,8},{10,11... | collective-permute-start | bytes 4718600 | tf_op jit(solution)/shard_map/ppermute | solution.py:27
  43.7 10.2 %collective-permute-start.9 = (bf16[480,256]{1,0:T(8,128)(2,1)S(1)}, bf16[480,256]{1,0:T(8,128)(2,1)S(1)}, u32[]{:S(2)}, u32[]{:S(2)}) collective-permute-start(bf16[480,256]{1,0:T(8,128)(2,1)S(1)} %shard_map.79.refs_0_.refs_7_), channel_id=1, source_target_pairs={{0,4},{4,8},{8,12},{12,16},{16,20},{20,24},{24,28},{28,0},{1,5},{5... | collective-permute-start | bytes 737288 | tf_op jit(solution)/shard_map/ppermute | solution.py:27
  43.8 10.2 %collective-permute-start.8 = (bf16[480,256]{1,0:T(8,128)(2,1)S(1)}, bf16[480,256]{1,0:T(8,128)(2,1)S(1)}, u32[]{:S(2)}, u32[]{:S(2)}) collective-permute-start(bf16[480,256]{1,0:T(8,128)(2,1)S(1)} %shard_map.79.refs_0_.refs_7_), channel_id=1, source_target_pairs={{0,28},{4,0},{8,4},{12,8},{16,12},{20,16},{24,20},{28,24},{1,29},{... | collective-permute-start | bytes 737288 | tf_op jit(solution)/shard_map/ppermute | solution.py:27
  48.1 20.5 %collective-permute-start.16 = (bf16[1600,256]{1,0:T(8,128)(2,1)S(1)}, bf16[1600,256]{1,0:T(8,128)(2,1)S(1)}, u32[]{:S(2)}, u32[]{:S(2)}) collective-permute-start(bf16[1600,256]{1,0:T(8,128)(2,1)S(1)} %shard_map.80.refs_0_.refs_17_), channel_id=1, source_target_pairs={{0,64},{64,128},{128,192},{192,0},{1,65},{65,129},{129,193},{193,1... | collective-permute-start | bytes 2457608 | tf_op jit(solution)/shard_map/ppermute | solution.py:27
  48.9 21.5 %collective-permute-start.15 = (bf16[1600,256]{1,0:T(8,128)(2,1)S(1)}, bf16[1600,256]{1,0:T(8,128)(2,1)S(1)}, u32[]{:S(2)}, u32[]{:S(2)}) collective-permute-start(bf16[1600,256]{1,0:T(8,128)(2,1)S(1)} %shard_map.80.refs_0_.refs_17_), channel_id=1, source_target_pairs={{0,192},{64,0},{128,64},{192,128},{1,193},{65,1},{129,65},{193,129... | collective-permute-start | bytes 2457608 | tf_op jit(solution)/shard_map/ppermute | solution.py:27
  50.4 1.1 %copy-start = (bf16[1536,256]{1,0:T(8,128)(2,1)S(1)}, bf16[1536,256]{1,0:T(8,128)(2,1)}, u32[]{:S(2)}) copy-start(bf16[1536,256]{1,0:T(8,128)(2,1)} %get-tuple-element.45.x) | copy-start | bytes 2359300
  53.9 7.9 %collective-permute-start.11 = (bf16[480,256]{1,0:T(8,128)(2,1)S(1)}, bf16[480,256]{1,0:T(8,128)(2,1)S(1)}, u32[]{:S(2)}, u32[]{:S(2)}) collective-permute-start(bf16[480,256]{1,0:T(8,128)(2,1)S(1)} %collective-permute-done.8.refs_1_.refs_8_), channel_id=1, source_target_pairs={{0,28},{4,0},{8,4},{12,8},{16,12},{20,16},{24,20},{28,24},{1,29},{... | collective-permute-start | bytes 737288 | tf_op jit(solution)/shard_map/ppermute | solution.py:27
  56.9 8.3 %collective-permute-start.12 = (bf16[480,256]{1,0:T(8,128)(2,1)S(1)}, bf16[480,256]{1,0:T(8,128)(2,1)S(1)}, u32[]{:S(2)}, u32[]{:S(2)}) collective-permute-start(bf16[480,256]{1,0:T(8,128)(2,1)S(1)} %collective-permute-done.9.refs_6_.refs_13_), channel_id=1, source_target_pairs={{0,4},{4,8},{8,12},{12,16},{16,20},{20,24},{24,28},{28,0},{1,5},{5... | collective-permute-start | bytes 737288 | tf_op jit(solution)/shard_map/ppermute | solution.py:27
  57.1 19.2 %collective-permute-start.21 = (bf16[1536,256]{1,0:T(8,128)(2,1)S(1)}, bf16[1536,256]{1,0:T(8,128)(2,1)S(1)}, u32[]{:S(2)}, u32[]{:S(2)}) collective-permute-start(bf16[1536,256]{1,0:T(8,128)(2,1)S(1)} %shard_map.81), channel_id=1, source_target_pairs={{0,2},{2,0},{1,3},{3,1},{4,6},{6,4},{5,7},{7,5},{8,10},{10,8},{9,1... | collective-permute-start | bytes 2359304 | tf_op jit(solution)/shard_map/ppermute | solution.py:27
  65.2 7.1 %collective-permute-start.13 = (bf16[480,256]{1,0:T(8,128)(2,1)S(1)}, bf16[480,256]{1,0:T(8,128)(2,1)S(1)}, u32[]{:S(2)}, u32[]{:S(2)}) collective-permute-start(bf16[480,256]{1,0:T(8,128)(2,1)S(1)} %collective-permute-done.11.refs_2_.refs_9_), channel_id=1, source_target_pairs={{0,28},{4,0},{8,4},{12,8},{16,12},{20,16},{24,20},{28,24},{1,29},{... | collective-permute-start | bytes 737288 | tf_op jit(solution)/shard_map/ppermute | solution.py:27
  65.5 7.4 %collective-permute-start.14 = (bf16[480,256]{1,0:T(8,128)(2,1)S(1)}, bf16[480,256]{1,0:T(8,128)(2,1)S(1)}, u32[]{:S(2)}, u32[]{:S(2)}) collective-permute-start(bf16[480,256]{1,0:T(8,128)(2,1)S(1)} %collective-permute-done.12.refs_5_.refs_12_), channel_id=1, source_target_pairs={{0,4},{4,8},{8,12},{12,16},{16,20},{20,24},{24,28},{28,0},{1,5},{5... | collective-permute-start | bytes 737288 | tf_op jit(solution)/shard_map/ppermute | solution.py:27
  68.6 10.7 %collective-permute-start.20 = (bf16[800,256]{1,0:T(8,128)(2,1)S(1)}, bf16[800,256]{1,0:T(8,128)(2,1)S(1)}, u32[]{:S(2)}, u32[]{:S(2)}) collective-permute-start(bf16[800,256]{1,0:T(8,128)(2,1)S(1)} %slice.33), channel_id=1, source_target_pairs={{0,64},{64,128},{128,192},{192,0},{1,65},{65,129},{129,193},{193,1... | collective-permute-start | bytes 1228808 | tf_op jit(solution)/shard_map/ppermute | solution.py:27
  70.5 5.8 %copy-start.1 = (bf16[1536,256]{1,0:T(8,128)(2,1)S(1)}, bf16[1536,256]{1,0:T(8,128)(2,1)}, u32[]{:S(2)}) copy-start(bf16[1536,256]{1,0:T(8,128)(2,1)} %get-tuple-element.60.own) | copy-start | bytes 2359300
  70.5 5.8 %copy-start.3 = (f32[128]{0:T(128)S(1)}, f32[128]{0:T(128)}, u32[]{:S(2)}) copy-start(f32[128]{0:T(128)} %param.7) | copy-start | bytes 1540
  70.5 11.6 %collective-permute-start.19 = (bf16[800,256]{1,0:T(8,128)(2,1)S(1)}, bf16[800,256]{1,0:T(8,128)(2,1)S(1)}, u32[]{:S(2)}, u32[]{:S(2)}) collective-permute-start(bf16[800,256]{1,0:T(8,128)(2,1)S(1)} %slice.32), channel_id=1, source_target_pairs={{0,192},{64,0},{128,64},{192,128},{1,193},{65,1},{129,65},{193,129... | collective-permute-start | bytes 1228808 | tf_op jit(solution)/shard_map/ppermute | solution.py:27
  72.9 9.2 %collective-permute-start.18 = (bf16[240,256]{1,0:T(8,128)(2,1)S(1)}, bf16[240,256]{1,0:T(8,128)(2,1)S(1)}, u32[]{:S(2)}, u32[]{:S(2)}) collective-permute-start(bf16[240,256]{1,0:T(8,128)(2,1)S(1)} %slice.25), channel_id=1, source_target_pairs={{0,4},{4,8},{8,12},{12,16},{16,20},{20,24},{24,28},{28,0},{1,5},{5... | collective-permute-start | bytes 368648 | tf_op jit(solution)/shard_map/ppermute | solution.py:27
  73.5 8.6 %collective-permute-start.17 = (bf16[240,256]{1,0:T(8,128)(2,1)S(1)}, bf16[240,256]{1,0:T(8,128)(2,1)S(1)}, u32[]{:S(2)}, u32[]{:S(2)}) collective-permute-start(bf16[240,256]{1,0:T(8,128)(2,1)S(1)} %slice.24), channel_id=1, source_target_pairs={{0,28},{4,0},{8,4},{12,8},{16,12},{20,16},{24,20},{28,24},{1,29},{... | collective-permute-start | bytes 368648 | tf_op jit(solution)/shard_map/ppermute | solution.py:27
where the time goes:
time: 86.2 us; the launch traced here: 86 us
  starting transfers between devices  41.1 us (48%)
  waiting for transfers between devices  21.9 us (25%)
  Pallas kernels  18.8 us (22%)
  local copies, waits for them, and re-layouts  2.1 us (2%)
  between operations  1.49 us (2%)
    ppermute x22, starting transfers between devices, shift(): return lax.ppermute(x, axis, [(i, (i + step) % n) for i in range(n)])  35.4 us
    ppermute x22, waiting for transfers between devices, shift(): return lax.ppermute(x, axis, [(i, (i + step) % n) for i in range(n)])  21.9 us
    pallas_call x1, Pallas kernels, project(): call(project_kernel, [jax.ShapeDtypeStruct((t, k * width), BF16) for k in...  9.06 us
    all_to_all x1, starting transfers between devices, body(): lax.all_to_all(line, ('yl', 'xh', 'xl', 'c'), split_axis=0, concat_axis=0...  5.75 us
    pallas_call x1, Pallas kernels, scale_last(): call(scale_last_kernel, [jax.ShapeDtypeStruct((2, 5120, 256), BF16), jax....  3.85 us
    pallas_call x2, Pallas kernels, scale_groups(): call(functools.partial(scale_groups_kernel, groups, offsets, n), [jax.Sha...  2.61 us
    unnamed x8, local copies, waits for them, and re-layouts  2.02 us
    pallas_call x1, Pallas kernels, finish(): call(finish_kernel, jax.ShapeDtypeStruct((t, width), BF16), flops=20 * t...  1.99 us
  transfers between devices with their start and end apart: 23, of which 13 were waited for; matrix products, arithmetic and copies ran while one was open for 1% of the time, Pallas kernels for 16%

commit v1 on v0

--- a/solution.py
+++ b/solution.py
@@ -292,93 +292,135 @@
     )(*ins)
 
 
-def scale_last_kernel(*refs):
-    z, y = lax.axis_index("z"), lax.axis_index(Y)
-    whole, half, low, high, part, extra = refs[:7], refs[7:14], *refs[14:17], refs[17:20]
-    far0, far1, bma, _, out, bm, held, acc, acc0 = refs[20:]
-    i = pl.program_id(0)
-
+def near_y(i):
+    return lax.rem(lax.axis_index(Y) + jnp.where(i == 2, 3, i), 4)
+
+
+def far_y(i):
+    return lax.rem(lax.axis_index(Y) + 2, 4)
+
+
+def put_in(out):
     def put(r, j, v):
         out[0, r * 128 : (r + 1) * 128, j * 128 : (j + 1) * 128] = v
 
+    return put
+
+
+def gather_rows(i, refs, held):
+    z = lax.axis_index("z")
+    whole, half, low, high, part = refs[:7], refs[7:14], *refs[14:17]
+    col = pl.multiple_of(i // 2 * 128, 128)
+
     def row(d):
         return pl.multiple_of(lax.rem(z + d, 8) * 80, 16)
 
-    def place(d, ref):
+    for d, ref, side in zip((0, 1, 2, 3, 5, 6, 7), whole, half):
         held[pl.ds(row(d), 80), :] = ref[...]
-
-    @pl.when(i == 0)
+        held[pl.ds(row(d) + 640, 80), 0:128] = side[:, pl.ds(col, 128)]
+    held[pl.ds(row(4) + 640, 80), 0:128] = part[:, pl.ds(col, 128)]
+
+    @pl.when(i < 3)
+    def _():
+        held[pl.ds(row(4), 80), :] = low[...]
+
+    @pl.when(i == 3)
+    def _():
+        held[pl.ds(row(4), 80), :] = high[...]
+
+
+def side_rows(ref, held):
+    held[640:960, 128:256] = ref[0:320, 0:128]
+    held[960:1280, 128:256] = ref[0:320, 128:256]
+
+
+def scale_near_kernel(*refs):
+    extra = refs[17:20]
+    _, out, acc, held = refs[20:]
+    step = pl.program_id(0)
+    i = near_y(step)
+
+    @pl.when(step == 0)
     def _():
         acc[...] = jnp.zeros_like(acc)
+
+    gather_rows(i, refs, held)
+    for k in range(3):
+
+        @pl.when(step == k)
+        def _(k=k):
+            side_rows(extra[k], held)
+
+    scale_blocks(held, 0, 1280, i * 10, put_in(out), acc)
+
+
+def scale_far_kernel(*refs):
+    far0, far1, bma, near, _, out, bm, held, acc, acc0 = refs[17:]
+    step = pl.program_id(0)
+    i = far_y(step)
+
+    @pl.when(step == 0)
+    def _():
+        acc[...] = near[...]
+        gather_rows(i, refs, held)
+        side_rows(far0, held)
+        scale_blocks(held, 0, 1280, i * 10, put_in(out), acc)
+
+    @pl.when(step == 1)
+    def _():
         acc0[...] = bma[...]
-
-    @pl.when(i < 4)
-    def _():
-        col = pl.multiple_of(i // 2 * 128, 128)
-        for d, ref, side in zip((0, 1, 2, 3, 5, 6, 7), whole, half):
-            place(d, ref)
-            held[pl.ds(row(d) + 640, 80), 0:128] = side[:, pl.ds(col, 128)]
-        held[pl.ds(row(4) + 640, 80), 0:128] = part[:, pl.ds(col, 128)]
-
-    @pl.when(i < 3)
-    def _():
-        place(4, low)
-
-    @pl.when(i == 3)
-    def _():
-        place(4, high)
-
-    for d, ref in zip((0, 1, 2, 3), (extra[0], extra[1], far0, extra[2])):
-
-        @pl.when((lax.rem(y + d, 4) == i) & (i < 4))
-        def _(ref=ref):
-            held[640:960, 128:256] = ref[0:320, 0:128]
-            held[960:1280, 128:256] = ref[0:320, 128:256]
-
-    @pl.when(i < 4)
-    def _():
-        scale_blocks(held, 0, 1280, i * 10, put, acc)
-
-    @pl.when(i == 4)
-    def _():
         held[0:480, :] = far0[320:800, :]
         held[480:1280, :] = far1[...]
-        scale_blocks(held, 0, 1280, lax.rem(y + 2, 4) * 10, put, acc0)
+        scale_blocks(held, 0, 1280, i * 10, put_in(out), acc0)
         bm[0] = acc0[:, :40]
         bm[1] = acc[:, :40]
 
 
-def scale_last(pieces, low, high, extra, far0, far1, done):
+def ring_specs(at):
     part = (80, 256)
-    at = lambda i: jnp.minimum(i, 3)
-    return call(
-        scale_last_kernel,
-        [jax.ShapeDtypeStruct((2, 5120, 256), BF16), jax.ShapeDtypeStruct((2, 2, 40), F32)],
-        flops=6400 * 256 * 8,
-        nbytes=6400 * 256 * 4,
-        grid=(5,),
-        in_specs=[pl.BlockSpec(part, lambda i: (at(i), 0))] * 7
+    return (
+        [pl.BlockSpec(part, lambda i: (at(i), 0))] * 7
         + [pl.BlockSpec(part, lambda i: (4 + lax.rem(at(i), 2), 0))] * 7
         + [
-            pl.BlockSpec(part, lambda i: (jnp.minimum(i, 2), 0)),
+            pl.BlockSpec(part, lambda i: (jnp.minimum(at(i), 2), 0)),
             pl.BlockSpec(part, lambda i: (0, 0)),
             pl.BlockSpec(part, lambda i: (1 + lax.rem(at(i), 2), 0)),
         ]
+    )
+
+
+def scale_near(ring, extra, buffer):
+    return call(
+        scale_near_kernel,
+        [jax.ShapeDtypeStruct((2, 5120, 256), BF16), jax.ShapeDtypeStruct((2, 128), F32)],
+        flops=3840 * 256 * 8,
+        nbytes=3840 * 256 * 4,
+        grid=(3,),
+        in_specs=ring_specs(near_y)
         + [pl.BlockSpec((320, 256), lambda i: (0, 0))] * 3
+        + [pl.BlockSpec(memory_space=pl.ANY)],
+        out_specs=[
+            pl.BlockSpec((1, 1280, 256), lambda i: (1, near_y(i), 0)),
+            pl.BlockSpec((2, 128), lambda i: (0, 0)),
+        ],
+        scratch_shapes=[pltpu.VMEM((1280, 256), BF16)],
+        input_output_aliases={20: 0},
+    )(*ring, *extra, buffer)
+
+
+def scale_far(ring, far0, far1, bma, near, buffer):
+    return call(
+        scale_far_kernel,
+        [jax.ShapeDtypeStruct((2, 5120, 256), BF16), jax.ShapeDtypeStruct((2, 2, 40), F32)],
+        flops=2560 * 256 * 8,
+        nbytes=2560 * 256 * 4,
+        grid=(2,),
+        in_specs=ring_specs(far_y)
         + [pl.BlockSpec((800, 256), lambda i: (0, 0))] * 2
-        + [
-            pl.BlockSpec((2, 128), lambda i: (0, 0)),
-            pl.BlockSpec(memory_space=pl.ANY),
-        ],
+        + [pl.BlockSpec((2, 128), lambda i: (0, 0))] * 2
+        + [pl.BlockSpec(memory_space=pl.ANY)],
         out_specs=[
-            pl.BlockSpec(
-                (1, 1280, 256),
-                lambda i: (
-                    jnp.where(i < 4, 1, 0),
-                    jnp.where(i < 4, i, lax.rem(lax.axis_index(Y) + 2, 4)),
-                    0,
-                ),
-            ),
+            pl.BlockSpec((1, 1280, 256), lambda i: (1 - i, far_y(i), 0)),
             pl.BlockSpec((2, 2, 40), lambda i: (0, 0, 0)),
         ],
         scratch_shapes=[
@@ -386,8 +428,8 @@
             pltpu.VMEM((2, 128), F32),
             pltpu.VMEM((2, 128), F32),
         ],
-        input_output_aliases={23: 0},
-    )(*pieces, *pieces, low, high, high, *extra, far0, far1, done[1], done[0])
+        input_output_aliases={21: 0},
+    )(*ring, far0, far1, bma, near, buffer)
 
 
 def body(activations, key_weight, key_gain, span_start, next_weight):
@@ -426,9 +468,12 @@
     high = shift(bz[5][240:], "z", 1)
     cosine, sine = tables(span_start[0], activations.shape[0])
     new_keys = finish(own, r1, r2, key_gain, cosine, sine)
-    low, high, far0, far1, new_keys, *done = after((low, high, far0, far1, new_keys, *done))
+    low, high, new_keys, *done = after((low, high, new_keys, *done))
     pieces = [bz[d] for d in (0, 1, 2, 3, 5, 6, 7)]
-    next_scaled, block_max = scale_last(pieces, low, high, [ma, up, down], far0, far1, done)
+    ring = [*pieces, *pieces, low, high, high]
+    buffer, near = scale_near(ring, [ma, up, down], done[0])
+    far0, far1, buffer, near = after((far0, far1, buffer, near))
+    next_scaled, block_max = scale_far(ring, far0, far1, done[1], near, buffer)
     return new_keys, next_scaled, block_max.transpose(0, 2, 1)
 
 

time: 86.2 us -> 88.6 us (1.028)
  starting transfers between devices: 41.1 us -> 42.3 us
    ppermute x22, starting transfers between devices: 35.4 us -> 36.6 us  [shift(): return lax.ppermute(x, axis, [(i, (i + step) % n) for i in range(n)])]
    pallas_call x1 -> x2, Pallas kernels: 3.85 us -> 4.29 us  [the longest x1 2.53 us: scale_near(): call(scale_near_kernel, [jax.ShapeDtypeStruct((2, 5120, 256), BF16), jax....]
  transfers between devices with their start and end apart: 23 -> 23, of which waited for: 13 -> 13; matrix products, arithmetic and copies ran while one was open for 1% -> 1% of each run, Pallas kernels for 16% -> 19%
where the time goes in v1:
time: 88.6 us; the launch traced here: 88.3 us
  starting transfers between devices  42.3 us (48%)
  waiting for transfers between devices  22.6 us (26%)
  Pallas kernels  19.2 us (22%)
  local copies, waits for them, and re-layouts  2.1 us (2%)
  between operations  1.51 us (2%)
    ppermute x22, starting transfers between devices, shift(): return lax.ppermute(x, axis, [(i, (i + step) % n) for i in range(n)])  36.6 us
    ppermute x22, waiting for transfers between devices, shift(): return lax.ppermute(x, axis, [(i, (i + step) % n) for i in range(n)])  22.6 us
    pallas_call x1, Pallas kernels, project(): call(project_kernel, [jax.ShapeDtypeStruct((t, k * width), BF16) for k in...  9.04 us
    all_to_all x1, starting transfers between devices, body(): lax.all_to_all(line, ('yl', 'xh', 'xl', 'c'), split_axis=0, concat_axis=0...  5.75 us
    pallas_call x2, Pallas kernels, scale_groups(): call(functools.partial(scale_groups_kernel, groups, offsets, n), [jax.Sha...  2.61 us
    pallas_call x1, Pallas kernels, scale_near(): call(scale_near_kernel, [jax.ShapeDtypeStruct((2, 5120, 256), BF16), jax....  2.53 us
    unnamed x8, local copies, waits for them, and re-layouts  2.02 us
    pallas_call x1, Pallas kernels, finish(): call(finish_kernel, jax.ShapeDtypeStruct((t, width), BF16), flops=20 * t...  1.99 us
  transfers between devices with their start and end apart: 23, of which 13 were waited for; matrix products, arithmetic and copies ran while one was open for 1% of the time, Pallas kernels for 19%

profile of v1, /device:TPU:26, one launch (start us, length us, event | category | flops | bytes accessed | tf_op | source)
XLA Modules:
  0.0 88.3 jit_solution(3660586293682670771)
XLA Ops:
  0.6 0.9 copy-done.2
  1.5 0.8 shard_map.76
  2.3 5.8 %all-to-all-start = ((bf16[16,40,256]{2,1,0:T(8,128)(2,1)}), bf16[16,40,256]{2,1,0:T(8,128)(2,1)S(1)}, u32[]{:S(2)}, u32[]{:S(2)}) async-start(bf16[16,40,256]{2,1,0:T(8,128)(2,1)} %shard_map.76), calls=%async_computation | async-start | bytes 655360 | tf_op jit(solution)/shard_map/all_to_all | solution.py:437
  8.1 9.0 %shard_map.77 = (bf16[1536,512]{1,0:T(8,128)(2,1)}, bf16[1536,256]{1,0:T(8,128)(2,1)}, bf16[1536,256]{1,0:T(8,128)(2,1)}) custom-call(bf16[1536,1280]{1,0:T(8,128)(2,1)} %a.1, bf16[1280,1024]{1,0:T(8,128)(2,1)} %w.1), custom_call_target="tpu_custom_call" | custom-call | flops 4026531840 | bytes 9699328 | tf_op jit(solution)/shard_map/pallas_call | solution.py:74
  17.2 5.9 %collective-permute-start.1 = (bf16[208,256]{1,0:T(8,128)(2,1)S(1)}, bf16[208,256]{1,0:T(8,128)(2,1)S(1)}, u32[]{:S(2)}, u32[]{:S(2)}) collective-permute-start(bf16[208,256]{1,0:T(8,128)(2,1)S(1)} %get-tuple-element.46.refs_0_), channel_id=1, source_target_pairs={{0,28},{4,0},{8,4},{12,8},{16,12},{20,16},{24,20},{28,24},{1,29},{... | collective-permute-start | bytes 319496 | tf_op jit(solution)/shard_map/ppermute | solution.py:27
  23.1 2.5 %collective-permute-done.1.refs_1_ = bf16[208,256]{1,0:T(8,128)(2,1)S(1)} collective-permute-done((bf16[208,256]{1,0:T(8,128)(2,1)S(1)}, bf16[208,256]{1,0:T(8,128)(2,1)S(1)}, u32[]{:S(2)}, u32[]{:S(2)}) %collective-permute-start.1) | collective-permute-done | bytes 106528 | tf_op jit(solution)/shard_map/ppermute | solution.py:27
  25.6 3.7 %collective-permute-start.2 = (bf16[208,256]{1,0:T(8,128)(2,1)S(1)}, bf16[208,256]{1,0:T(8,128)(2,1)S(1)}, u32[]{:S(2)}, u32[]{:S(2)}) collective-permute-start(bf16[208,256]{1,0:T(8,128)(2,1)S(1)} %collective-permute-done.1.refs_1_), channel_id=1, source_target_pairs={{0,28},{4,0},{8,4},{12,8},{16,12},{20,16},{24,20},{28,24},{1,29},{... | collective-permute-start | bytes 319496 | tf_op jit(solution)/shard_map/ppermute | solution.py:27
  29.3 2.3 %collective-permute-done.2.refs_2_ = bf16[208,256]{1,0:T(8,128)(2,1)S(1)} collective-permute-done((bf16[208,256]{1,0:T(8,128)(2,1)S(1)}, bf16[208,256]{1,0:T(8,128)(2,1)S(1)}, u32[]{:S(2)}, u32[]{:S(2)}) %collective-permute-start.2) | collective-permute-done | bytes 106528 | tf_op jit(solution)/shard_map/ppermute | solution.py:27
  31.6 3.6 %collective-permute-start.3 = (bf16[208,256]{1,0:T(8,128)(2,1)S(1)}, bf16[208,256]{1,0:T(8,128)(2,1)S(1)}, u32[]{:S(2)}, u32[]{:S(2)}) collective-permute-start(bf16[208,256]{1,0:T(8,128)(2,1)S(1)} %collective-permute-done.2.refs_2_), channel_id=1, source_target_pairs={{0,28},{4,0},{8,4},{12,8},{16,12},{20,16},{24,20},{28,24},{1,29},{... | collective-permute-start | bytes 319496 | tf_op jit(solution)/shard_map/ppermute | solution.py:27
  35.2 1.2 %collective-permute-start = (bf16[256,256]{1,0:T(8,128)(2,1)S(1)}, bf16[256,256]{1,0:T(8,128)(2,1)S(1)}, u32[]{:S(2)}, u32[]{:S(2)}) collective-permute-start(bf16[256,256]{1,0:T(8,128)(2,1)S(1)} %get-tuple-element.45.own), channel_id=1, source_target_pairs={{0,128},{128,0},{1,129},{129,1},{2,130},{130,2},{3,131},{131,3},{4... | collective-permute-start | bytes 393224 | tf_op jit(solution)/shard_map/ppermute | solution.py:27
  36.5 1.0 %collective-permute-done.3.refs_3_ = bf16[208,256]{1,0:T(8,128)(2,1)S(1)} collective-permute-done((bf16[208,256]{1,0:T(8,128)(2,1)S(1)}, bf16[208,256]{1,0:T(8,128)(2,1)S(1)}, u32[]{:S(2)}, u32[]{:S(2)}) %collective-permute-start.3) | collective-permute-done | bytes 106528 | tf_op jit(solution)/shard_map/ppermute | solution.py:27
  37.5 3.6 %collective-permute-start.4 = (bf16[208,256]{1,0:T(8,128)(2,1)S(1)}, bf16[208,256]{1,0:T(8,128)(2,1)S(1)}, u32[]{:S(2)}, u32[]{:S(2)}) collective-permute-start(bf16[208,256]{1,0:T(8,128)(2,1)S(1)} %collective-permute-done.3.refs_3_), channel_id=1, source_target_pairs={{0,28},{4,0},{8,4},{12,8},{16,12},{20,16},{24,20},{28,24},{1,29},{... | collective-permute-start | bytes 319496 | tf_op jit(solution)/shard_map/ppermute | solution.py:27
  42.4 1.1 %collective-permute-done.4.refs_4_ = bf16[208,256]{1,0:T(8,128)(2,1)S(1)} collective-permute-done((bf16[208,256]{1,0:T(8,128)(2,1)S(1)}, bf16[208,256]{1,0:T(8,128)(2,1)S(1)}, u32[]{:S(2)}, u32[]{:S(2)}) %collective-permute-start.4) | collective-permute-done | bytes 106528 | tf_op jit(solution)/shard_map/ppermute | solution.py:27
  43.7 3.7 %collective-permute-start.8 = (bf16[480,256]{1,0:T(8,128)(2,1)S(1)}, bf16[480,256]{1,0:T(8,128)(2,1)S(1)}, u32[]{:S(2)}, u32[]{:S(2)}) collective-permute-start(bf16[480,256]{1,0:T(8,128)(2,1)S(1)} %shard_map.79.refs_0_.refs_7_), channel_id=1, source_target_pairs={{0,28},{4,0},{8,4},{12,8},{16,12},{20,16},{24,20},{28,24},{1,29},{... | collective-permute-start | bytes 737288 | tf_op jit(solution)/shard_map/ppermute | solution.py:27
  48.0 0.8 collective-permute-start.15
  48.8 2.7 %collective-permute-start.16 = (bf16[1600,256]{1,0:T(8,128)(2,1)S(1)}, bf16[1600,256]{1,0:T(8,128)(2,1)S(1)}, u32[]{:S(2)}, u32[]{:S(2)}) collective-permute-start(bf16[1600,256]{1,0:T(8,128)(2,1)S(1)} %shard_map.80.refs_0_.refs_17_), channel_id=1, source_target_pairs={{0,64},{64,128},{128,192},{192,0},{1,65},{65,129},{129,193},{193,1... | collective-permute-start | bytes 2457608 | tf_op jit(solution)/shard_map/ppermute | solution.py:27
  51.5 1.1 %copy-done = bf16[1536,256]{1,0:T(8,128)(2,1)S(1)} copy-done((bf16[1536,256]{1,0:T(8,128)(2,1)S(1)}, bf16[1536,256]{1,0:T(8,128)(2,1)}, u32[]{:S(2)}) %copy-start) | copy-done | bytes 786456
  53.2 3.4 %collective-permute-done.9.refs_6_.refs_13_ = bf16[480,256]{1,0:T(8,128)(2,1)S(1)} collective-permute-done((bf16[480,256]{1,0:T(8,128)(2,1)S(1)}, bf16[480,256]{1,0:T(8,128)(2,1)S(1)}, u32[]{:S(2)}, u32[]{:S(2)}) %collective-permute-start.9) | collective-permute-done | bytes 245792 | tf_op jit(solution)/shard_map/ppermute | solution.py:27
  56.9 1.7 %collective-permute-start.12 = (bf16[480,256]{1,0:T(8,128)(2,1)S(1)}, bf16[480,256]{1,0:T(8,128)(2,1)S(1)}, u32[]{:S(2)}, u32[]{:S(2)}) collective-permute-start(bf16[480,256]{1,0:T(8,128)(2,1)S(1)} %collective-permute-done.9.refs_6_.refs_13_), channel_id=1, source_target_pairs={{0,4},{4,8},{8,12},{12,16},{16,20},{20,24},{24,28},{28,0},{1,5},{5... | collective-permute-start | bytes 737288 | tf_op jit(solution)/shard_map/ppermute | solution.py:27
  58.8 0.6 collective-permute-start.19
  59.5 1.1 %shard_map.82 = (bf16[2,5120,256]{2,1,0:T(8,128)(2,1)}, f32[2,128]{1,0:T(2,128)S(1)}) custom-call(bf16[1600,256]{1,0:T(8,128)(2,1)S(1)} %shard_map.80.refs_0_.refs_17_), custom_call_target="tpu_custom_call" | custom-call | flops 2621440 | bytes 1310720 | tf_op jit(solution)/shard_map/pallas_call | solution.py:280
  60.7 3.1 %collective-permute-done.11.refs_2_.refs_9_ = bf16[480,256]{1,0:T(8,128)(2,1)S(1)} collective-permute-done((bf16[480,256]{1,0:T(8,128)(2,1)S(1)}, bf16[480,256]{1,0:T(8,128)(2,1)S(1)}, u32[]{:S(2)}, u32[]{:S(2)}) %collective-permute-start.11) | collective-permute-done | bytes 245792 | tf_op jit(solution)/shard_map/ppermute | solution.py:27
  63.8 1.5 %collective-permute-done.12.refs_5_.refs_12_ = bf16[480,256]{1,0:T(8,128)(2,1)S(1)} collective-permute-done((bf16[480,256]{1,0:T(8,128)(2,1)S(1)}, bf16[480,256]{1,0:T(8,128)(2,1)S(1)}, u32[]{:S(2)}, u32[]{:S(2)}) %collective-permute-start.12) | collective-permute-done | bytes 245792 | tf_op jit(solution)/shard_map/ppermute | solution.py:27
  65.6 1.7 %collective-permute-start.14 = (bf16[480,256]{1,0:T(8,128)(2,1)S(1)}, bf16[480,256]{1,0:T(8,128)(2,1)S(1)}, u32[]{:S(2)}, u32[]{:S(2)}) collective-permute-start(bf16[480,256]{1,0:T(8,128)(2,1)S(1)} %collective-permute-done.12.refs_5_.refs_12_), channel_id=1, source_target_pairs={{0,4},{4,8},{8,12},{12,16},{16,20},{20,24},{24,28},{28,0},{1,5},{5... | collective-permute-start | bytes 737288 | tf_op jit(solution)/shard_map/ppermute | solution.py:27
  67.6 2.2 %collective-permute-done.15.refs_0_.refs_18_ = bf16[1600,256]{1,0:T(8,128)(2,1)S(1)} collective-permute-done((bf16[1600,256]{1,0:T(8,128)(2,1)S(1)}, bf16[1600,256]{1,0:T(8,128)(2,1)S(1)}, u32[]{:S(2)}, u32[]{:S(2)}) %collective-permute-start.15) | collective-permute-done | bytes 819232 | tf_op jit(solution)/shard_map/ppermute | solution.py:27
  70.0 3.3 %collective-permute-start.21 = (bf16[800,256]{1,0:T(8,128)(2,1)S(1)}, bf16[800,256]{1,0:T(8,128)(2,1)S(1)}, u32[]{:S(2)}, u32[]{:S(2)}) collective-permute-start(bf16[800,256]{1,0:T(8,128)(2,1)S(1)} %slice.33), channel_id=1, source_target_pairs={{0,64},{64,128},{128,192},{192,0},{1,65},{65,129},{129,193},{193,1... | collective-permute-start | bytes 1228808 | tf_op jit(solution)/shard_map/ppermute | solution.py:27
  73.2 1.5 %shard_map.83 = (bf16[2,5120,256]{2,1,0:T(8,128)(2,1)}, f32[2,128]{1,0:T(2,128)S(1)}) custom-call(bf16[1600,256]{1,0:T(8,128)(2,1)S(1)} %collective-permute-done.15.refs_0_.refs_18_, bf16[1600,256]{1,0:T(8,128)(2,1)S(1)} %collective-permute-done.16.refs_1_.refs_19_, ...), custom_call_target="tpu_custom_call", output_to_operand_aliasing={{0}: (3, {}), {1}: (2, {})} | custom-call | flops 5242880 | bytes 2621440 | tf_op jit(solution)/shard_map/pallas_call | solution.py:280
  74.8 3.0 %collective-permute-start.17 = (bf16[240,256]{1,0:T(8,128)(2,1)S(1)}, bf16[240,256]{1,0:T(8,128)(2,1)S(1)}, u32[]{:S(2)}, u32[]{:S(2)}) collective-permute-start(bf16[240,256]{1,0:T(8,128)(2,1)S(1)} %slice.24), channel_id=1, source_target_pairs={{0,28},{4,0},{8,4},{12,8},{16,12},{20,16},{24,20},{28,24},{1,29},{... | collective-permute-start | bytes 368648 | tf_op jit(solution)/shard_map/ppermute | solution.py:27
  78.0 2.0 %shard_map.84 = bf16[1536,256]{1,0:T(8,128)(2,1)} custom-call(bf16[1536,256]{1,0:T(8,128)(2,1)S(1)} %copy-done.1, bf16[1536,512]{1,0:T(8,128)(2,1)S(1)} %collective-permute-done.10.r.r1, bf16[1536,256]{1,0:T(8,128)(2,1)S(1)} %collective-permute-done.19.r2, f32[1,128]{1,0:T(1,128)S(1)} %bitcast.10, f32[1536,128]{1,0:T(8,128)S(1)} %bitcast.8, ...), custom_call_target="tpu_custom_call" | custom-call | flops 7864320 | bytes 5505024 | tf_op jit(solution)/shard_map/pallas_call | solution.py:124
  80.2 3.7 %collective-permute-done.18.refs_15_.refs_16_ = bf16[240,256]{1,0:T(8,128)(2,1)S(1)} collective-permute-done((bf16[240,256]{1,0:T(8,128)(2,1)S(1)}, bf16[240,256]{1,0:T(8,128)(2,1)S(1)}, u32[]{:S(2)}, u32[]{:S(2)}) %collective-permute-start.18) | collective-permute-done | bytes 122912 | tf_op jit(solution)/shard_map/ppermute | solution.py:27
  84.0 2.5 %shard_map.85 = (bf16[2,5120,256]{2,1,0:T(8,128)(2,1)}, f32[2,128]{1,0:T(2,128)S(1)}) custom-call(bf16[480,256]{1,0:T(8,128)(2,1)S(1)} %shard_map.79.refs_0_.refs_7_, bf16[480,256]{1,0:T(8,128)(2,1)S(1)} %collective-permute-done.8.refs_1_.refs_8_, bf16[480,256]{1,0:T(8,128)(2,1)S(1)} %collective-permute-done.11.refs_2_.refs_9_, ...), custom_call_target="tpu_custom_call", output_to_operand_aliasing={{0}: (20, {})} | custom-call | flops 7864320 | bytes 3932160 | tf_op jit(solution)/shard_map/pallas_call | solution.py:393
  86.5 1.8 %shard_map.86 = (bf16[2,5120,256]{2,1,0:T(8,128)(2,1)}, f32[2,2,40]{2,1,0:T(2,128)}) custom-call(bf16[480,256]{1,0:T(8,128)(2,1)S(1)} %shard_map.79.refs_0_.refs_7_, bf16[480,256]{1,0:T(8,128)(2,1)S(1)} %collective-permute-done.8.refs_1_.refs_8_, bf16[480,256]{1,0:T(8,128)(2,1)S(1)} %collective-permute-done.11.refs_2_.refs_9_, ...), custom_call_target="tpu_custom_call", output_to_operand_aliasing={{0}: (21, {})} | custom-call | flops 5242880 | bytes 2621440 | tf_op jit(solution)/shard_map/pallas_call | solution.py:412
  (47 shorter events, 3.6 us)
Async XLA Ops:
  0.6 0.9 %copy-start.2 = (bf16[2,20,1024]{2,0,1:T(2,128)(2,1)S(1)}, bf16[2,20,1024]{2,0,1:T(2,128)(2,1)}, u32[]{:S(2)}) copy-start(bf16[2,20,1024]{2,0,1:T(2,128)(2,1)} %param.9) | copy-start | bytes 245764
  2.3 14.8 %all-to-all-start = ((bf16[16,40,256]{2,1,0:T(8,128)(2,1)}), bf16[16,40,256]{2,1,0:T(8,128)(2,1)S(1)}, u32[]{:S(2)}, u32[]{:S(2)}) async-start(bf16[16,40,256]{2,1,0:T(8,128)(2,1)} %shard_map.76), calls=%async_computation | async-start | bytes 655360 | tf_op jit(solution)/shard_map/all_to_all | solution.py:437
  17.2 8.5 %collective-permute-start.1 = (bf16[208,256]{1,0:T(8,128)(2,1)S(1)}, bf16[208,256]{1,0:T(8,128)(2,1)S(1)}, u32[]{:S(2)}, u32[]{:S(2)}) collective-permute-start(bf16[208,256]{1,0:T(8,128)(2,1)S(1)} %get-tuple-element.46.refs_0_), channel_id=1, source_target_pairs={{0,28},{4,0},{8,4},{12,8},{16,12},{20,16},{24,20},{28,24},{1,29},{... | collective-permute-start | bytes 319496 | tf_op jit(solution)/shard_map/ppermute | solution.py:27
  23.1 6.2 %collective-permute-start.5 = (bf16[208,256]{1,0:T(8,128)(2,1)S(1)}, bf16[208,256]{1,0:T(8,128)(2,1)S(1)}, u32[]{:S(2)}, u32[]{:S(2)}) collective-permute-start(bf16[208,256]{1,0:T(8,128)(2,1)S(1)} %get-tuple-element.46.refs_0_), channel_id=1, source_target_pairs={{0,4},{4,8},{8,12},{12,16},{16,20},{20,24},{24,28},{28,0},{1,5},{5... | collective-permute-start | bytes 319496 | tf_op jit(solution)/shard_map/ppermute | solution.py:27
  25.6 6.0 %collective-permute-start.2 = (bf16[208,256]{1,0:T(8,128)(2,1)S(1)}, bf16[208,256]{1,0:T(8,128)(2,1)S(1)}, u32[]{:S(2)}, u32[]{:S(2)}) collective-permute-start(bf16[208,256]{1,0:T(8,128)(2,1)S(1)} %collective-permute-done.1.refs_1_), channel_id=1, source_target_pairs={{0,28},{4,0},{8,4},{12,8},{16,12},{20,16},{24,20},{28,24},{1,29},{... | collective-permute-start | bytes 319496 | tf_op jit(solution)/shard_map/ppermute | solution.py:27
  29.3 7.2 %collective-permute-start.6 = (bf16[208,256]{1,0:T(8,128)(2,1)S(1)}, bf16[208,256]{1,0:T(8,128)(2,1)S(1)}, u32[]{:S(2)}, u32[]{:S(2)}) collective-permute-start(bf16[208,256]{1,0:T(8,128)(2,1)S(1)} %collective-permute-done.5.refs_7_), channel_id=1, source_target_pairs={{0,4},{4,8},{8,12},{12,16},{16,20},{20,24},{24,28},{28,0},{1,5},{5... | collective-permute-start | bytes 319496 | tf_op jit(solution)/shard_map/ppermute | solution.py:27
  31.6 5.9 %collective-permute-start.3 = (bf16[208,256]{1,0:T(8,128)(2,1)S(1)}, bf16[208,256]{1,0:T(8,128)(2,1)S(1)}, u32[]{:S(2)}, u32[]{:S(2)}) collective-permute-start(bf16[208,256]{1,0:T(8,128)(2,1)S(1)} %collective-permute-done.2.refs_2_), channel_id=1, source_target_pairs={{0,28},{4,0},{8,4},{12,8},{16,12},{20,16},{24,20},{28,24},{1,29},{... | collective-permute-start | bytes 319496 | tf_op jit(solution)/shard_map/ppermute | solution.py:27
  35.2 6.5 %collective-permute-start = (bf16[256,256]{1,0:T(8,128)(2,1)S(1)}, bf16[256,256]{1,0:T(8,128)(2,1)S(1)}, u32[]{:S(2)}, u32[]{:S(2)}) collective-permute-start(bf16[256,256]{1,0:T(8,128)(2,1)S(1)} %get-tuple-element.45.own), channel_id=1, source_target_pairs={{0,128},{128,0},{1,129},{129,1},{2,130},{130,2},{3,131},{131,3},{4... | collective-permute-start | bytes 393224 | tf_op jit(solution)/shard_map/ppermute | solution.py:27
  36.5 5.9 %collective-permute-start.7 = (bf16[208,256]{1,0:T(8,128)(2,1)S(1)}, bf16[208,256]{1,0:T(8,128)(2,1)S(1)}, u32[]{:S(2)}, u32[]{:S(2)}) collective-permute-start(bf16[208,256]{1,0:T(8,128)(2,1)S(1)} %collective-permute-done.6.refs_6_), channel_id=1, source_target_pairs={{0,4},{4,8},{8,12},{12,16},{16,20},{20,24},{24,28},{28,0},{1,5},{5... | collective-permute-start | bytes 319496 | tf_op jit(solution)/shard_map/ppermute | solution.py:27
  37.5 5.9 %collective-permute-start.4 = (bf16[208,256]{1,0:T(8,128)(2,1)S(1)}, bf16[208,256]{1,0:T(8,128)(2,1)S(1)}, u32[]{:S(2)}, u32[]{:S(2)}) collective-permute-start(bf16[208,256]{1,0:T(8,128)(2,1)S(1)} %collective-permute-done.3.refs_3_), channel_id=1, source_target_pairs={{0,28},{4,0},{8,4},{12,8},{16,12},{20,16},{24,20},{28,24},{1,29},{... | collective-permute-start | bytes 319496 | tf_op jit(solution)/shard_map/ppermute | solution.py:27
  43.6 8.0 %collective-permute-start.10 = (bf16[1536,512]{1,0:T(8,128)(2,1)}, bf16[1536,512]{1,0:T(8,128)(2,1)S(1)}, u32[]{:S(2)}, u32[]{:S(2)}) collective-permute-start(bf16[1536,512]{1,0:T(8,128)(2,1)} %get-tuple-element.50), channel_id=1, source_target_pairs={{0,1},{1,0},{2,3},{3,2},{4,5},{5,4},{6,7},{7,6},{8,9},{9,8},{10,11... | collective-permute-start | bytes 4718600 | tf_op jit(solution)/shard_map/ppermute | solution.py:27
  43.7 9.5 %collective-permute-start.8 = (bf16[480,256]{1,0:T(8,128)(2,1)S(1)}, bf16[480,256]{1,0:T(8,128)(2,1)S(1)}, u32[]{:S(2)}, u32[]{:S(2)}) collective-permute-start(bf16[480,256]{1,0:T(8,128)(2,1)S(1)} %shard_map.79.refs_0_.refs_7_), channel_id=1, source_target_pairs={{0,28},{4,0},{8,4},{12,8},{16,12},{20,16},{24,20},{28,24},{1,29},{... | collective-permute-start | bytes 737288 | tf_op jit(solution)/shard_map/ppermute | solution.py:27
  47.4 9.2 %collective-permute-start.9 = (bf16[480,256]{1,0:T(8,128)(2,1)S(1)}, bf16[480,256]{1,0:T(8,128)(2,1)S(1)}, u32[]{:S(2)}, u32[]{:S(2)}) collective-permute-start(bf16[480,256]{1,0:T(8,128)(2,1)S(1)} %shard_map.79.refs_0_.refs_7_), channel_id=1, source_target_pairs={{0,4},{4,8},{8,12},{12,16},{16,20},{20,24},{24,28},{28,0},{1,5},{5... | collective-permute-start | bytes 737288 | tf_op jit(solution)/shard_map/ppermute | solution.py:27
  48.0 21.8 %collective-permute-start.15 = (bf16[1600,256]{1,0:T(8,128)(2,1)S(1)}, bf16[1600,256]{1,0:T(8,128)(2,1)S(1)}, u32[]{:S(2)}, u32[]{:S(2)}) collective-permute-start(bf16[1600,256]{1,0:T(8,128)(2,1)S(1)} %shard_map.80.refs_0_.refs_17_), channel_id=1, source_target_pairs={{0,192},{64,0},{128,64},{192,128},{1,193},{65,1},{129,65},{193,129... | collective-permute-start | bytes 2457608 | tf_op jit(solution)/shard_map/ppermute | solution.py:27
  48.8 21.1 %collective-permute-start.16 = (bf16[1600,256]{1,0:T(8,128)(2,1)S(1)}, bf16[1600,256]{1,0:T(8,128)(2,1)S(1)}, u32[]{:S(2)}, u32[]{:S(2)}) collective-permute-start(bf16[1600,256]{1,0:T(8,128)(2,1)S(1)} %shard_map.80.refs_0_.refs_17_), channel_id=1, source_target_pairs={{0,64},{64,128},{128,192},{192,0},{1,65},{65,129},{129,193},{193,1... | collective-permute-start | bytes 2457608 | tf_op jit(solution)/shard_map/ppermute | solution.py:27
  51.5 1.1 %copy-start = (bf16[1536,256]{1,0:T(8,128)(2,1)S(1)}, bf16[1536,256]{1,0:T(8,128)(2,1)}, u32[]{:S(2)}) copy-start(bf16[1536,256]{1,0:T(8,128)(2,1)} %get-tuple-element.49.x) | copy-start | bytes 2359300
  56.6 7.2 %collective-permute-start.11 = (bf16[480,256]{1,0:T(8,128)(2,1)S(1)}, bf16[480,256]{1,0:T(8,128)(2,1)S(1)}, u32[]{:S(2)}, u32[]{:S(2)}) collective-permute-start(bf16[480,256]{1,0:T(8,128)(2,1)S(1)} %collective-permute-done.8.refs_1_.refs_8_), channel_id=1, source_target_pairs={{0,28},{4,0},{8,4},{12,8},{16,12},{20,16},{24,20},{28,24},{1,29},{... | collective-permute-start | bytes 737288 | tf_op jit(solution)/shard_map/ppermute | solution.py:27
  56.9 8.4 %collective-permute-start.12 = (bf16[480,256]{1,0:T(8,128)(2,1)S(1)}, bf16[480,256]{1,0:T(8,128)(2,1)S(1)}, u32[]{:S(2)}, u32[]{:S(2)}) collective-permute-start(bf16[480,256]{1,0:T(8,128)(2,1)S(1)} %collective-permute-done.9.refs_6_.refs_13_), channel_id=1, source_target_pairs={{0,4},{4,8},{8,12},{12,16},{16,20},{20,24},{24,28},{28,0},{1,5},{5... | collective-permute-start | bytes 737288 | tf_op jit(solution)/shard_map/ppermute | solution.py:27
  58.8 19.1 %collective-permute-start.19 = (bf16[1536,256]{1,0:T(8,128)(2,1)S(1)}, bf16[1536,256]{1,0:T(8,128)(2,1)S(1)}, u32[]{:S(2)}, u32[]{:S(2)}) collective-permute-start(bf16[1536,256]{1,0:T(8,128)(2,1)S(1)} %shard_map.81), channel_id=1, source_target_pairs={{0,2},{2,0},{1,3},{3,1},{4,6},{6,4},{5,7},{7,5},{8,10},{10,8},{9,1... | collective-permute-start | bytes 2359304 | tf_op jit(solution)/shard_map/ppermute | solution.py:27
  65.3 9.4 %collective-permute-start.13 = (bf16[480,256]{1,0:T(8,128)(2,1)S(1)}, bf16[480,256]{1,0:T(8,128)(2,1)S(1)}, u32[]{:S(2)}, u32[]{:S(2)}) collective-permute-start(bf16[480,256]{1,0:T(8,128)(2,1)S(1)} %collective-permute-done.11.refs_2_.refs_9_), channel_id=1, source_target_pairs={{0,28},{4,0},{8,4},{12,8},{16,12},{20,16},{24,20},{28,24},{1,29},{... | collective-permute-start | bytes 737288 | tf_op jit(solution)/shard_map/ppermute | solution.py:27
  65.6 9.1 %collective-permute-start.14 = (bf16[480,256]{1,0:T(8,128)(2,1)S(1)}, bf16[480,256]{1,0:T(8,128)(2,1)S(1)}, u32[]{:S(2)}, u32[]{:S(2)}) collective-permute-start(bf16[480,256]{1,0:T(8,128)(2,1)S(1)} %collective-permute-done.12.refs_5_.refs_12_), channel_id=1, source_target_pairs={{0,4},{4,8},{8,12},{12,16},{16,20},{20,24},{24,28},{28,0},{1,5},{5... | collective-permute-start | bytes 737288 | tf_op jit(solution)/shard_map/ppermute | solution.py:27
  67.6 10.4 %copy-start.1 = (bf16[1536,256]{1,0:T(8,128)(2,1)S(1)}, bf16[1536,256]{1,0:T(8,128)(2,1)}, u32[]{:S(2)}) copy-start(bf16[1536,256]{1,0:T(8,128)(2,1)} %get-tuple-element.64.own) | copy-start | bytes 2359300
  67.6 10.4 %copy-start.3 = (f32[128]{0:T(128)S(1)}, f32[128]{0:T(128)}, u32[]{:S(2)}) copy-start(f32[128]{0:T(128)} %param.7) | copy-start | bytes 1540
  69.8 16.7 %collective-permute-start.20 = (bf16[800,256]{1,0:T(8,128)(2,1)S(1)}, bf16[800,256]{1,0:T(8,128)(2,1)S(1)}, u32[]{:S(2)}, u32[]{:S(2)}) collective-permute-start(bf16[800,256]{1,0:T(8,128)(2,1)S(1)} %slice.32), channel_id=1, source_target_pairs={{0,192},{64,0},{128,64},{192,128},{1,193},{65,1},{129,65},{193,129... | collective-permute-start | bytes 1228808 | tf_op jit(solution)/shard_map/ppermute | solution.py:27
  70.0 16.5 %collective-permute-start.21 = (bf16[800,256]{1,0:T(8,128)(2,1)S(1)}, bf16[800,256]{1,0:T(8,128)(2,1)S(1)}, u32[]{:S(2)}, u32[]{:S(2)}) collective-permute-start(bf16[800,256]{1,0:T(8,128)(2,1)S(1)} %slice.33), channel_id=1, source_target_pairs={{0,64},{64,128},{128,192},{192,0},{1,65},{65,129},{129,193},{193,1... | collective-permute-start | bytes 1228808 | tf_op jit(solution)/shard_map/ppermute | solution.py:27
  74.8 5.5 %collective-permute-start.17 = (bf16[240,256]{1,0:T(8,128)(2,1)S(1)}, bf16[240,256]{1,0:T(8,128)(2,1)S(1)}, u32[]{:S(2)}, u32[]{:S(2)}) collective-permute-start(bf16[240,256]{1,0:T(8,128)(2,1)S(1)} %slice.24), channel_id=1, source_target_pairs={{0,28},{4,0},{8,4},{12,8},{16,12},{20,16},{24,20},{28,24},{1,29},{... | collective-permute-start | bytes 368648 | tf_op jit(solution)/shard_map/ppermute | solution.py:27
  77.8 6.2 %collective-permute-start.18 = (bf16[240,256]{1,0:T(8,128)(2,1)S(1)}, bf16[240,256]{1,0:T(8,128)(2,1)S(1)}, u32[]{:S(2)}, u32[]{:S(2)}) collective-permute-start(bf16[240,256]{1,0:T(8,128)(2,1)S(1)} %slice.25), channel_id=1, source_target_pairs={{0,4},{4,8},{8,12},{12,16},{16,20},{20,24},{24,28},{28,0},{1,5},{5... | collective-permute-start | bytes 368648 | tf_op jit(solution)/shard_map/ppermute | solution.py:27
